TPU v7x, 256 devices: a whole 4x4x8 slice. The times are simulated.
256 devices in a mesh: ctx: 32 (over y, z), tp: 8 (over x, core).
Axes of the slice: x: 4, y: 4, z: 8, core: 2. Of those that a mesh axis runs over, the one named last changes fastest.
Arguments:
- context_block_rows: bfloat16 [16384, 8192], P('ctx', 'tp'), may hold values from -16 to 16
- query_hidden_rows: bfloat16 [64, 8192], P(None, 'tp'), may hold values from -16 to 16
- query_token_positions: int32 [64], replicated, may hold values from 16384 to 16573, as said below
- query_bound: int32 [64], replicated, may hold values from 1 to 16384, as said below
- query_matrix: bfloat16 [8192, 8192], P('ctx', 'tp'), may hold values from -0.0625 to 0.0625
- key_matrix: bfloat16 [8192, 1024], P('ctx', 'tp'), may hold values from -0.0625 to 0.0625
- value_matrix: bfloat16 [8192, 1024], P('ctx', 'tp'), may hold values from -0.0625 to 0.0625
Outputs:
- block_out: bfloat16 [16384, 8192], P('ctx', 'tp')
- query_out: bfloat16 [64, 8192], P(None, 'tp')
Inputs may be any that keep to these rules, and one draw needn't show every extreme that they name: query_token_positions rise strictly with the index; the first is 16384 and the last 16573. `query_bound`: some query token sees all 16384 context tokens.
All inputs are finite; a program needn't handle non-finite values.
Results may differ from a plain program's by a relative error of at most 0.0059.
The roundings to bfloat16 on the way count: a program that leaves them out, or rounds other values in their place, can miss the bound.
Values may be sent and summed in bfloat16 or wider, within the bound.
A program may use at most 128 MiB of HBM per device.

v0:
```python
import math
import jax
import jax.numpy as jnp
from jax import lax
from jax.sharding import PartitionSpec as P

HEAD_SIZE = 128


def from_root(value, axis, source):
    kept = jnp.where(lax.axis_index(axis) == source, value, 0).astype(value.dtype)
    return lax.psum(kept, axis)


def rope_table(half):
    values = []
    for index in range(half):
        freq = 500000.0 ** (-2.0 * index / (2.0 * half))
        wavelen = 2.0 * math.pi / freq
        if wavelen > 8192.0:
            values.append(freq / 8.0)
        elif wavelen < 2048.0:
            values.append(freq)
        else:
            smooth = (8192.0 / wavelen - 1.0) / 3.0
            values.append((1.0 - smooth) * freq / 8.0 + smooth * freq)
    return values


def apply_rotary(values, token_positions):
    half = values.shape[-1] // 2
    freqs = jnp.asarray(rope_table(half), jnp.float32)
    angle = token_positions.astype(jnp.float32)[:, None] * freqs[None, :]
    cosine = jnp.cos(angle)[:, None, :]
    sine = jnp.sin(angle)[:, None, :]
    first = values[..., :half]
    second = values[..., half:]
    return jnp.concatenate([first * cosine - second * sine, second * cosine + first * sine], -1)


def attend(query_heads_split, keys, values, valid):
    scale = 1.0 / math.sqrt(query_heads_split.shape[-1])
    scores = (
        jnp.einsum("qkgd,skd->qkgs", query_heads_split, keys, preferred_element_type=jnp.float32)
        * scale
    )
    scores = jnp.where(valid[:, None, None, :], scores, -1e30)
    peak = jnp.max(scores, -1)
    weights = jnp.exp(scores - peak[..., None])
    total = jnp.sum(weights, -1)
    mixed = jnp.einsum(
        "qkgs,skd->qkgd", weights.astype(jnp.bfloat16), values, preferred_element_type=jnp.float32
    )
    return (peak, total, mixed)


def on_device(
    context_block_rows,
    query_hidden_rows,
    query_token_positions,
    query_bound,
    query_matrix,
    key_matrix,
    value_matrix,
):
    ctx_index = lax.axis_index("ctx")
    blk = context_block_rows.shape[0]
    qcount = query_hidden_rows.shape[0]
    heads_q = query_matrix.shape[1] // HEAD_SIZE
    heads_kv = key_matrix.shape[1] // HEAD_SIZE
    head_group = heads_q // heads_kv
    whole_rows, whole_query = (
        lax.all_gather(context_block_rows, "tp", axis=1, tiled=True),
        lax.all_gather(query_hidden_rows, "tp", axis=1, tiled=True),
    )
    stacked = jnp.concatenate([whole_rows, whole_query], 0)
    head_rows = blk + qcount
    proj_query = jnp.dot(
        stacked,
        lax.all_gather(query_matrix, "ctx", axis=0, tiled=True),
        preferred_element_type=jnp.float32,
    )
    proj_key = jnp.dot(
        stacked,
        lax.all_gather(key_matrix, "ctx", axis=0, tiled=True),
        preferred_element_type=jnp.float32,
    )
    proj_value = jnp.dot(
        stacked,
        lax.all_gather(value_matrix, "ctx", axis=0, tiled=True),
        preferred_element_type=jnp.float32,
    )
    local_pos = ctx_index * blk + jnp.arange(blk, dtype=jnp.int32)
    k_block = apply_rotary(proj_key[:blk].reshape(blk, heads_kv, HEAD_SIZE), local_pos).astype(
        jnp.bfloat16
    )
    v_block = proj_value[:blk].reshape(blk, heads_kv, HEAD_SIZE).astype(jnp.bfloat16)
    key_token_rows = apply_rotary(
        proj_key[blk:head_rows].reshape(qcount, heads_kv, HEAD_SIZE), query_token_positions
    ).astype(jnp.bfloat16)
    value_token_rows = (
        proj_value[blk:head_rows].reshape(qcount, heads_kv, HEAD_SIZE).astype(jnp.bfloat16)
    )
    anchor_key, anchor_value = (from_root(k_block, "ctx", 0), from_root(v_block, "ctx", 0))
    q_block = apply_rotary(proj_query[:blk].reshape(blk, heads_q, HEAD_SIZE), local_pos).astype(
        jnp.bfloat16
    )
    query_token_rows = (
        apply_rotary(proj_query[blk:].reshape(qcount, heads_q, HEAD_SIZE), query_token_positions)
        .astype(jnp.bfloat16)
        .reshape(qcount, heads_kv, head_group, HEAD_SIZE)
    )
    keys_cat = jnp.concatenate([anchor_key, k_block], 0)
    values_cat = jnp.concatenate([anchor_value, v_block], 0)
    anchor_live = ctx_index > 0
    rows_step = min(blk, 512)
    rows_here = 0 + jnp.arange(rows_step, dtype=jnp.int32)
    valid = jnp.concatenate(
        [
            jnp.broadcast_to(anchor_live, (rows_step, blk)),
            rows_here[:, None] >= jnp.arange(blk, dtype=jnp.int32)[None, :],
        ],
        1,
    )
    query_heads_split = q_block.reshape(rows_step, heads_kv, head_group, HEAD_SIZE)
    peak, total, mixed = attend(query_heads_split, keys_cat, values_cat, valid)
    outputs = (
        (mixed / total[..., None]).astype(jnp.bfloat16).reshape(rows_step, heads_q * HEAD_SIZE)
    )
    valid_ctx = local_pos[None, :] < query_bound[:, None]
    peak, total, mixed = attend(query_token_rows, k_block, v_block, valid_ctx)
    top = lax.pmax(peak, "ctx")
    scaled = jnp.exp(peak - top)
    total_all, mixed_all = lax.psum((total * scaled, mixed * scaled[..., None]), "ctx")
    own = jnp.arange(qcount, dtype=jnp.int32)
    self_peak, self_total, self_mixed = attend(
        query_token_rows, key_token_rows, value_token_rows, own[:, None] >= own[None, :]
    )
    final = jnp.maximum(top, self_peak)
    w_ctx = jnp.exp(top - final)
    w_self = jnp.exp(self_peak - final)
    query_out = (mixed_all * w_ctx[..., None] + self_mixed * w_self[..., None]) / (
        total_all * w_ctx + self_total * w_self
    )[..., None]
    query_out = query_out.astype(jnp.bfloat16).reshape(qcount, heads_q * HEAD_SIZE)
    return (outputs, query_out)


def solution(mesh):
    placed = (
        P("ctx", "tp"),
        P(None, "tp"),
        P(),
        P(),
        P("ctx", "tp"),
        P("ctx", "tp"),
        P("ctx", "tp"),
    )
    return jax.shard_map(
        on_device,
        mesh=mesh,
        in_specs=placed,
        out_specs=(P("ctx", "tp"), P(None, "tp")),
        check_vma=False,
    )
```

profile of v0, /device:TPU:2, one launch (start us, length us, event | category | flops | bytes accessed | tf_op | source)
XLA Modules:
  0.0 689.7 jit_solution(3943614140132584248)
XLA Ops:
  7.2 0.0 all-gather.6.cloned.1.call-start
  7.2 0.7 all-gather.6.cloned.1.call-update
  7.9 0.0 all-gather.8.cloned.1.call-start
  7.9 0.7 all-gather.8.cloned.1.call-update
  8.6 0.0 all-gather.12.cloned.1.call-start
  8.7 0.7 all-gather.12.cloned.1.call-update
  9.4 0.0 all-gather.10.cloned.1.call-start
  9.4 0.5 all-gather.10.cloned.1.call-update
  10.0 0.0 all-gather.14.cloned.1.call-start
  10.0 0.5 all-gather.14.cloned.1.call-update
  10.5 0.0 all-reduce.7.cloned.1.call-start
  10.6 0.7 convert_element_type.69
  11.3 0.1 iota_compare_fusion
  11.3 0.9 concatenate.62
  12.3 1.4 broadcast_compare_fusion
  13.6 0.8 multiply_cosine_fusion.3
  14.5 2.5 multiply_cosine_fusion
  17.0 47.3 %all-gather.6.cloned.1.call-done = bf16[512,8192]{1,0:T(8,128)(2,1)} async-done(((bf16[512,1024]{1,0:T(8,128)(2,1)}), bf16[512,8192]{1,0:T(8,128)(2,1)}) %all-gather.6.cloned.1.call-update) | async-done | bytes 8388624 | tf_op jit(solution)/shard_map/all_gather | solution.py:73
  64.3 7.6 %constant_dynamic-update-slice_fusion.1 = bf16[576,8192]{1,0:T(8,128)(2,1)} fusion(bf16[512,8192]{1,0:T(8,128)(2,1)} %all-gather.6.cloned.1.call-done), kind=kLoop, calls=%fused_computation.100 | loop fusion | bytes 16777216
  71.9 19.5 %all-gather.8.cloned.1.call-done = bf16[64,8192]{1,0:T(8,128)(2,1)} async-done(((bf16[64,1024]{1,0:T(8,128)(2,1)}), bf16[64,8192]{1,0:T(8,128)(2,1)}) %all-gather.8.cloned.1.call-update) | async-done | bytes 1048592 | tf_op jit(solution)/shard_map/all_gather | solution.py:74
  91.4 2.3 constant_dynamic-update-slice_fusion
  93.7 79.8 %all-gather.12.cloned.1.call-done = bf16[8192,128]{1,0:T(8,128)(2,1)} async-done(((bf16[256,128]{1,0:T(8,128)(2,1)}), bf16[8192,128]{1,0:T(8,128)(2,1)}) %all-gather.12.cloned.1.call-update) | async-done | bytes 2097168 | tf_op jit(solution)/shard_map/all_gather | solution.py:85
  173.5 5.8 fusion.83
  179.4 0.0 copy-done.9
  179.4 1.2 fusion.35
  180.6 0.0 copy-start.1
  180.6 0.8 maximum_select_fusion
  181.4 0.8 fusion.64
  182.2 68.9 %all-gather.10.cloned.1.call-done = bf16[8192,128]{1,0:T(8,128)(2,1)} async-done(((bf16[256,128]{1,0:T(8,128)(2,1)}), bf16[8192,128]{1,0:T(8,128)(2,1)}) %all-gather.10.cloned.1.call-update) | async-done | bytes 2097168 | tf_op jit(solution)/shard_map/all_gather | solution.py:90
  251.1 6.9 convolution_convert_fusion
  258.0 0.0 copy-start.2
  258.0 0.7 slice_bitcast_fusion.3
  258.8 0.0 all-reduce.7.cloned.1.call-update
  258.8 0.0 all-reduce.5.cloned.1.call-start
  258.9 132.5 %all-gather.14.cloned.1.call-done = bf16[8192,1024]{1,0:T(8,128)(2,1)} async-done(((bf16[256,1024]{1,0:T(8,128)(2,1)}), bf16[8192,1024]{1,0:T(8,128)(2,1)}) %all-gather.14.cloned.1.call-update) | async-done | bytes 16777232 | tf_op jit(solution)/shard_map/all_gather | solution.py:80
  391.4 0.0 copy-done.2
  391.4 14.9 %fusion.84 = f32[576,1024]{1,0:T(8,128)S(1)} fusion(bf16[576,8192]{1,0:T(8,128)(2,1)} %constant_dynamic-update-slice_fusion, bf16[8192,1024]{1,0:T(8,128)(2,1)} %all-gather.14.cloned.1.call-done), kind=kOutput, calls=%fused_computation.126 | convolution fusion | flops 9663676416 | bytes 28573696 | tf_op jit(solution)/shard_map/dot_general | solution.py:78
  406.4 0.1 slice_bitcast_fusion
  406.6 0.1 fusion.80
  406.7 0.1 subtract_convert_fusion.1
  406.8 1.4 fusion.81
  408.2 1.0 fusion.25
  409.1 71.4 %pmax.7 = f32[64,1,8]{0,2,1:T(8,128)S(1)} all-reduce(f32[64,1,8]{0,2,1:T(8,128)S(1)} %bitcast.169), channel_id=1, replica_groups=mesh['ctx'=32,'tp'=8] {'ctx'}, use_global_device_ids=true, to_apply=%region_5.6 | all-reduce | flops 512 | bytes 4096 | tf_op jit(solution)/shard_map/pmax | solution.py:132
  480.6 0.0 copy-start.7
  480.6 0.5 copy.38
  481.1 2.0 fusion.79
  483.1 0.0 copy-done.7
  483.1 0.6 bitcast_multiply_fusion.1
  483.7 1.1 fusion.14
  484.7 0.0 all-reduce.5.cloned.1.call-update
  484.8 3.5 subtract_convert_fusion
  488.2 47.8 %all-reduce.7.cloned.1.call-done = (bf16[512,1,128]{2,0,1:T(8,128)(2,1)}, bf16[512,1,128]{2,0,1:T(8,128)(2,1)}) async-done(((bf16[512,1,128]{2,0,1:T(8,128)(2,1)}, bf16[512,1,128]{2,0,1:T(8,128)(2,1)}), (bf16[512,1,128]{2,0,1:T(8,128)(2,1)}, bf16[512,1,128]{2,0,1:T(8,128)(2,1)})) %all-reduce.7.cloned.1.call-update) | async-done | bytes 262160 | tf_op jit(solution)/shard_map/psum | solution.py:12
  536.1 10.7 %fusion.2 = (f32[512,8]{0,1:T(8,128)S(1)}, f32[1024,512,8]{1,0,2:T(8,128)}) fusion(pred[512,1024]{0,1:T(8,128)(4,1)} %concatenate.62, bf16[512,8,64]{2,0,1:T(8,128)(2,1)} %get-tuple-element.9, bf16[512,8,64]{2,0,1:T(8,128)(2,1)S(1)} %get-tuple-element.8, bf16[512,1,64]{2,0,1:T(8,128)(2,1)} %copy-done.1, bf16[512,1,64]{2,0,1:T(8,128)(2,1)S(1)} %get-tuple-element.14, ...), kind=kOutput, calls=%fused_computation.4 | convolution fusion | flops 1089204224 | bytes 18628608 | tf_op jit(solution)/shard_map/qkgd,skd->qkgs/dot_general | solution.py:44
  546.8 0.0 copy-done
  546.8 9.3 %fusion = f32[512,8]{0,1:T(8,128)S(1)} fusion(f32[1024,512,8]{1,0,2:T(8,128)} %get-tuple-element.32, f32[512,8]{0,1:T(8,128)S(1)} %get-tuple-element.31, pred[512,1024]{0,1:T(8,128)(4,1)S(1)} %copy-done), kind=kLoop, calls=%fused_computation.2 | loop fusion | flops 16773120 | bytes 17334272 | tf_op jit(solution)/shard_map/reduce_sum | solution.py:50
  556.1 0.3 fusion.82
  556.5 9.1 %fusion.7 = bf16[1,128,512,8]{2,1,3,0:T(8,128)(2,1)S(1)} fusion(f32[1024,512,8]{1,0,2:T(8,128)} %get-tuple-element.32, f32[512,8]{0,1:T(8,128)S(1)} %get-tuple-element.31, pred[512,1024]{0,1:T(8,128)(4,1)S(1)} %copy-done, f32[512,8]{0,1:T(8,128)S(1)} %fusion, bf16[512,1,128]{2,0,1:T(8,128)(2,1)S(1)} %copy-done.4, bf16[512,1,128]{2,0,1:T(8,128)(2,1)S(1)} %copy-done.10), kind=kOutput, calls=%fused_computation.10 | convolution fusion | flops 1092091904 | bytes 18644992 | tf_op jit(solution)/shard_map/qkgs,skd->qkgd/dot_general | solution.py:51
  565.6 0.1 fusion.44
  565.7 1.3 copy.29
  567.0 72.5 %psum.31 = f32[64,1,8]{0,2,1:T(8,128)S(1)} all-reduce(f32[64,1,8]{0,2,1:T(8,128)S(1)} %copy-done.8), channel_id=1, replica_groups=mesh['ctx'=32,'tp'=8] {'ctx'}, use_global_device_ids=true, to_apply=%region_9.10 | all-reduce | flops 512 | bytes 4096 | tf_op jit(solution)/shard_map/psum | solution.py:134
  639.5 41.2 %all-reduce.5.cloned.1.call-done = f32[64,1,8,128]{3,0,2,1:T(8,128)} async-done(((f32[64,1,8,128]{3,0,2,1:T(8,128)}), f32[64,1,8,128]{3,0,2,1:T(8,128)}) %all-reduce.5.cloned.1.call-update) | async-done | bytes 262160 | tf_op jit(solution)/shard_map/psum | solution.py:134
  680.7 1.3 fusion.19
  682.0 0.1 copy.28
  682.1 0.7 copy.50
  (23 shorter events, 0.1 us)
Async XLA Ops:
  7.2 57.1 %all-gather.6.cloned.1.call-start = ((), (), s32[]{:S(2)}) async-start(), calls=%async_computation | async-start | bytes 9437184 | tf_op jit(solution)/shard_map/all_gather | solution.py:73
  7.9 83.5 %all-gather.8.cloned.1.call-start = ((), (), s32[]{:S(2)}) async-start(), calls=%async_computation.1 | async-start | bytes 1179648 | tf_op jit(solution)/shard_map/all_gather | solution.py:74
  8.6 164.9 %all-gather.12.cloned.1.call-start = ((), (), s32[]{:S(2)}) async-start(), calls=%async_computation.3 | async-start | bytes 2162688 | tf_op jit(solution)/shard_map/all_gather | solution.py:85
  9.4 241.7 %all-gather.10.cloned.1.call-start = ((), (), s32[]{:S(2)}) async-start(), calls=%async_computation.2 | async-start | bytes 2162688 | tf_op jit(solution)/shard_map/all_gather | solution.py:90
  10.0 381.4 %all-gather.14.cloned.1.call-start = ((), (), s32[]{:S(2)}) async-start(), calls=%async_computation.4 | async-start | bytes 17301504 | tf_op jit(solution)/shard_map/all_gather | solution.py:80
  10.5 525.5 %all-reduce.7.cloned.1.call-start = ((), (), s32[]{:S(2)}) async-start(), calls=%async_computation.6 | async-start | bytes 524288 | tf_op jit(solution)/shard_map/psum | solution.py:12
  71.9 107.5 %copy-start.9 = (f32[64]{0:T(128)S(1)}, f32[64]{0:T(128)}, u32[]{:S(2)}) copy-start(f32[64]{0:T(128)} %constant.24.clone) | copy-start | bytes 772
  180.6 225.7 %copy-start.1 = (bf16[512,1,64]{2,0,1:T(8,128)(2,1)}, bf16[512,1,64]{2,0,1:T(8,128)(2,1)S(1)}, u32[]{:S(2)}) copy-start(bf16[512,1,64]{2,0,1:T(8,128)(2,1)S(1)} %get-tuple-element.15) | copy-start | bytes 196612
  258.0 133.4 %copy-start.2 = (bf16[576,128]{1,0:T(8,128)(2,1)}, bf16[576,128]{1,0:T(8,128)(2,1)S(1)}, u32[]{:S(2)}) copy-start(bf16[576,128]{1,0:T(8,128)(2,1)S(1)} %convolution_convert_fusion) | copy-start | bytes 442372
  258.8 421.9 %all-reduce.5.cloned.1.call-start = ((), (), s32[]{:S(2)}) async-start(), calls=%async_computation.5 | async-start | bytes 524288 | tf_op jit(solution)/shard_map/psum | solution.py:134
  480.6 2.5 copy-start.7
  480.6 3.1 copy-start.3
  536.1 10.7 %copy-start = (pred[512,1024]{0,1:T(8,128)(4,1)S(1)}, pred[512,1024]{0,1:T(8,128)(4,1)}, u32[]{:S(2)}) copy-start(pred[512,1024]{0,1:T(8,128)(4,1)} %concatenate.62) | copy-start | bytes 1572868
  546.8 9.3 %copy-start.5 = (bf16[64,64]{1,0:T(8,128)(2,1)S(1)}, bf16[64,64]{1,0:T(8,128)(2,1)}, u32[]{:S(2)}) copy-start(bf16[64,64]{1,0:T(8,128)(2,1)} %get-tuple-element.20) | copy-start | bytes 24580
  546.8 9.3 %copy-start.6 = (bf16[64,64]{1,0:T(8,128)(2,1)S(1)}, bf16[64,64]{1,0:T(8,128)(2,1)}, u32[]{:S(2)}) copy-start(bf16[64,64]{1,0:T(8,128)(2,1)} %get-tuple-element.21) | copy-start | bytes 24580
  546.8 9.6 %copy-start.4 = (bf16[512,1,128]{2,0,1:T(8,128)(2,1)S(1)}, bf16[512,1,128]{2,0,1:T(8,128)(2,1)}, u32[]{:S(2)}) copy-start(bf16[512,1,128]{2,0,1:T(8,128)(2,1)} %get-tuple-element.18) | copy-start | bytes 393220
  546.8 9.6 %copy-start.10 = (bf16[512,1,128]{2,0,1:T(8,128)(2,1)S(1)}, bf16[512,1,128]{2,0,1:T(8,128)(2,1)}, u32[]{:S(2)}) copy-start(bf16[512,1,128]{2,0,1:T(8,128)(2,1)} %get-tuple-element.7) | copy-start | bytes 393220
  556.5 10.5 %copy-start.8 = (f32[64,1,8]{0,2,1:T(8,128)S(1)}, f32[64,1,8]{0,2,1:T(8,128)}, u32[]{:S(2)}) copy-start(f32[64,1,8]{0,2,1:T(8,128)} %get-tuple-element.25) | copy-start | bytes 6148
Sparse Core Ops, SparseCore 0:
  9.8 54.4 all-gather.5
  66.1 25.2 all-gather.7
  94.0 79.4 all-gather.11
  176.0 75.1 all-gather.9
  253.6 137.7 all-gather.13
  394.7 141.2 all-reduce.6
  539.5 141.1 all-reduce.4
where the time goes:
time: 690 us
  waiting for transfers between devices  440 us (64%)
  blocking collectives  144 us (21%)
  matrix products  51.5 us (7%)
  other arithmetic  23.5 us (3%)
  local copies, waits for them, and re-layouts  15.8 us (2%)
  between operations  14.4 us (2%)
    all_gather x1, waiting for transfers between devices, on_device(): lax.all_gather(query_matrix, 'ctx', axis=0, tiled=True)  133 us
    all_gather x1, waiting for transfers between devices, on_device(): lax.all_gather(key_matrix, 'ctx', axis=0, tiled=True)  79.8 us
    psum x1, blocking collectives, on_device(): lax.psum((total * scaled, mixed * scaled[..., None]), 'ctx')  72.5 us
    pmax x1, blocking collectives, on_device(): top = lax.pmax(peak, 'ctx')  71.4 us
    all_gather x1, waiting for transfers between devices, on_device(): lax.all_gather(value_matrix, 'ctx', axis=0, tiled=True)  68.9 us
    psum x1, waiting for transfers between devices, from_root(): return lax.psum(kept, axis)  47.8 us
    all_gather x1, waiting for transfers between devices, on_device(): lax.all_gather(context_block_rows, 'tp', axis=1, tiled=True)  47.3 us
    psum x1, waiting for transfers between devices, on_device(): lax.psum((total * scaled, mixed * scaled[..., None]), 'ctx')  41.2 us
  transfers between devices with their start and end apart: 7, of which 7 were waited for; matrix products, arithmetic and copies ran while one was open for 13% of the time, Pallas kernels for 0%

commit v1 on v0

--- a/solution.py
+++ b/solution.py
@@ -69,9 +69,23 @@
     heads_q = query_matrix.shape[1] // HEAD_SIZE
     heads_kv = key_matrix.shape[1] // HEAD_SIZE
     head_group = heads_q // heads_kv
+
+    def recast_tracks(my_data, chip_axis):
+        res = lax.axis_size(chip_axis)
+        plain = lax.axis_index(chip_axis)
+        w2, now = (res, plain)
+        tall, passed = (my_data, 1)
+        while passed < w2:
+            piece_now = lax.ppermute(tall, chip_axis, [(ix, ix ^ passed) for ix in range(w2)])
+            a_next = jnp.concatenate([tall, piece_now], 1)
+            b_next = jnp.concatenate([piece_now, tall], axis=1)
+            tall = jnp.where(now & passed == 0, a_next, b_next)
+            passed = 2 * passed
+        return tall
+
     whole_rows, whole_query = (
         lax.all_gather(context_block_rows, "tp", axis=1, tiled=True),
-        lax.all_gather(query_hidden_rows, "tp", axis=1, tiled=True),
+        recast_tracks(query_hidden_rows, "tp"),
     )
     stacked = jnp.concatenate([whole_rows, whole_query], 0)
     head_rows = blk + qcount

time: 690 us -> 662 us (0.959)
  waiting for transfers between devices: 440 us -> 415 us
  local copies, waits for them, and re-layouts: 15.8 us -> 5.88 us
    all_gather x1, waiting for transfers between devices: 79.8 us -> 54.4 us  [on_device(): lax.all_gather(key_matrix, 'ctx', axis=0, tiled=True)]
    all_gather x1 -> x0, waiting for transfers between devices: 19.5 us -> none  [on_device(): lax.all_gather(query_hidden_rows, 'tp', axis=1, tiled=True)]
    ppermute x0 -> x3, waiting for transfers between devices: none -> 15.1 us  [recast_tracks(): lax.ppermute(tall, chip_axis, [(ix, ix ^ passed) for ix in range(w2)])]
    unnamed x29 -> x28, local copies, waits for them, and re-layouts: 10.3 us -> 2.72 us
  transfers between devices with their start and end apart: 7 -> 9, of which waited for: 7 -> 9; matrix products, arithmetic and copies ran while one was open for 13% -> 12% of each run, Pallas kernels for 0% -> 0%
where the time goes in v1:
time: 662 us
  waiting for transfers between devices  415 us (63%)
  blocking collectives  144 us (22%)
  matrix products  53.5 us (8%)
  other arithmetic  24.9 us (4%)
  between operations  14.4 us (2%)
    all_gather x1, waiting for transfers between devices, on_device(): lax.all_gather(query_matrix, 'ctx', axis=0, tiled=True)  133 us
    psum x1, blocking collectives, on_device(): lax.psum((total * scaled, mixed * scaled[..., None]), 'ctx')  72.5 us
    all_gather x1, waiting for transfers between devices, on_device(): lax.all_gather(value_matrix, 'ctx', axis=0, tiled=True)  71.5 us
    pmax x1, blocking collectives, on_device(): top = lax.pmax(peak, 'ctx')  71.2 us
    all_gather x1, waiting for transfers between devices, on_device(): lax.all_gather(key_matrix, 'ctx', axis=0, tiled=True)  54.4 us
    all_gather x1, waiting for transfers between devices, on_device(): lax.all_gather(context_block_rows, 'tp', axis=1, tiled=True)  50.5 us
    psum x1, waiting for transfers between devices, from_root(): return lax.psum(kept, axis)  47.2 us
    psum x1, waiting for transfers between devices, on_device(): lax.psum((total * scaled, mixed * scaled[..., None]), 'ctx')  41 us
  transfers between devices with their start and end apart: 9, of which 9 were waited for; matrix products, arithmetic and copies ran while one was open for 12% of the time, Pallas kernels for 0%

profile of v1, /device:TPU:2, one launch (start us, length us, event | category | flops | bytes accessed | tf_op | source)
XLA Modules:
  0.0 662.0 jit_solution(17620882640962045848)
XLA Ops:
  7.2 0.0 all-gather.9.cloned.1.call-start
  7.2 0.7 all-gather.9.cloned.1.call-update
  7.9 0.0 all-gather.5.cloned.1.call-start
  7.9 0.7 all-gather.5.cloned.1.call-update
  8.6 0.0 all-gather.7.cloned.1.call-start
  8.7 0.7 all-gather.7.cloned.1.call-update
  9.4 0.0 all-gather.11.cloned.1.call-start
  9.4 0.5 all-gather.11.cloned.1.call-update
  10.0 0.0 all-reduce.7.cloned.1.call-start
  10.0 0.1 collective-permute-start
  10.1 0.1 iota_compare_fusion
  10.2 1.4 collective-permute-done
  11.6 1.0 maximum_select_fusion.2
  12.7 2.4 collective-permute-start.1
  15.1 0.7 convert_element_type.69
  15.7 0.9 concatenate.86
  16.6 1.4 broadcast_compare_fusion
  18.0 3.7 collective-permute-done.1
  21.7 0.1 maximum_select_fusion.1
  21.8 1.7 collective-permute-start.2
  23.5 0.8 multiply_cosine_fusion.3
  24.3 2.5 multiply_cosine_fusion
  26.8 10.0 %collective-permute-done.2 = bf16[64,4096]{1,0:T(8,128)(2,1)S(1)} collective-permute-done((bf16[64,4096]{1,0:T(8,128)(2,1)S(1)}, bf16[64,4096]{1,0:T(8,128)(2,1)S(1)}, u32[]{:S(2)}, u32[]{:S(2)}) %collective-permute-start.2) | collective-permute-done | bytes 524320 | tf_op jit(solution)/shard_map/ppermute | solution.py:79
  36.9 0.2 maximum_select_fusion
  37.1 0.0 copy-start.9
  37.1 54.4 %all-gather.9.cloned.1.call-done = bf16[8192,128]{1,0:T(8,128)(2,1)} async-done(((bf16[256,128]{1,0:T(8,128)(2,1)}), bf16[8192,128]{1,0:T(8,128)(2,1)}) %all-gather.9.cloned.1.call-update) | async-done | bytes 2097168 | tf_op jit(solution)/shard_map/all_gather | solution.py:99
  91.5 50.5 %all-gather.5.cloned.1.call-done = bf16[512,8192]{1,0:T(8,128)(2,1)} async-done(((bf16[512,1024]{1,0:T(8,128)(2,1)}), bf16[512,8192]{1,0:T(8,128)(2,1)}) %all-gather.5.cloned.1.call-update) | async-done | bytes 8388624 | tf_op jit(solution)/shard_map/all_gather | solution.py:87
  142.0 7.1 %fusion.8 = f32[576,128]{1,0:T(8,128)S(1)} fusion(bf16[8192,128]{1,0:T(8,128)(2,1)} %all-gather.9.cloned.1.call-done, bf16[64,8192]{1,0:T(8,128)(2,1)S(1)} %maximum_select_fusion, bf16[512,8192]{1,0:T(8,128)(2,1)} %all-gather.5.cloned.1.call-done), kind=kOutput, calls=%fused_computation.10 | convolution fusion | flops 1226833920 | bytes 11829248 | tf_op jit(solution)/shard_map/dot_general | solution.py:97
  149.2 1.2 fusion.39
  150.4 0.0 copy-start.1
  150.5 0.8 maximum_select_fusion.3
  151.2 0.8 fusion.68
  152.0 71.5 %all-gather.7.cloned.1.call-done = bf16[8192,128]{1,0:T(8,128)(2,1)} async-done(((bf16[256,128]{1,0:T(8,128)(2,1)}), bf16[8192,128]{1,0:T(8,128)(2,1)}) %all-gather.7.cloned.1.call-update) | async-done | bytes 2097168 | tf_op jit(solution)/shard_map/all_gather | solution.py:104
  223.6 6.6 fusion.22
  230.2 0.8 slice_bitcast_fusion.3
  230.9 0.0 all-reduce.7.cloned.1.call-update
  231.0 0.2 all-reduce.5.cloned.1.call-start
  231.2 132.6 %all-gather.11.cloned.1.call-done = bf16[8192,1024]{1,0:T(8,128)(2,1)} async-done(((bf16[256,1024]{1,0:T(8,128)(2,1)}), bf16[8192,1024]{1,0:T(8,128)(2,1)}) %all-gather.11.cloned.1.call-update) | async-done | bytes 16777232 | tf_op jit(solution)/shard_map/all_gather | solution.py:94
  363.8 15.8 %fusion.7 = f32[576,1024]{1,0:T(8,128)S(1)} fusion(bf16[8192,1024]{1,0:T(8,128)(2,1)} %all-gather.11.cloned.1.call-done, bf16[64,8192]{1,0:T(8,128)(2,1)S(1)} %maximum_select_fusion, bf16[512,8192]{1,0:T(8,128)(2,1)} %all-gather.5.cloned.1.call-done), kind=kOutput, calls=%fused_computation.9 | convolution fusion | flops 9682550784 | bytes 28573696 | tf_op jit(solution)/shard_map/dot_general | solution.py:92
  379.7 0.1 slice_bitcast_fusion
  379.9 0.1 fusion.87
  380.1 0.1 subtract_convert_fusion.1
  380.2 1.4 fusion.88
  381.6 1.0 fusion.29
  382.5 71.2 %pmax.7 = f32[64,1,8]{0,2,1:T(8,128)S(1)} all-reduce(f32[64,1,8]{0,2,1:T(8,128)S(1)} %bitcast.166), channel_id=1, replica_groups=mesh['ctx'=32,'tp'=8] {'ctx'}, use_global_device_ids=true, to_apply=%region_5.6 | all-reduce | flops 512 | bytes 4096 | tf_op jit(solution)/shard_map/pmax | solution.py:146
  453.8 0.5 copy.38
  454.3 2.0 fusion.86
  456.3 0.6 bitcast_multiply_fusion.1
  456.9 1.1 fusion.17
  457.9 0.0 all-reduce.5.cloned.1.call-update
  457.9 3.5 subtract_convert_fusion
  461.4 47.2 %all-reduce.7.cloned.1.call-done = (bf16[512,1,128]{2,0,1:T(8,128)(2,1)}, bf16[512,1,128]{2,0,1:T(8,128)(2,1)}) async-done(((bf16[512,1,128]{2,0,1:T(8,128)(2,1)}, bf16[512,1,128]{2,0,1:T(8,128)(2,1)}), (bf16[512,1,128]{2,0,1:T(8,128)(2,1)}, bf16[512,1,128]{2,0,1:T(8,128)(2,1)})) %all-reduce.7.cloned.1.call-update) | async-done | bytes 262160 | tf_op jit(solution)/shard_map/psum | solution.py:12
  508.6 10.7 %fusion.2 = (f32[512,8]{0,1:T(8,128)S(1)}, f32[1024,512,8]{1,0,2:T(8,128)}) fusion(pred[512,1024]{0,1:T(8,128)(4,1)} %concatenate.86, bf16[512,8,64]{2,0,1:T(8,128)(2,1)} %get-tuple-element.9, bf16[512,8,64]{2,0,1:T(8,128)(2,1)S(1)} %get-tuple-element.8, bf16[512,1,64]{2,0,1:T(8,128)(2,1)} %copy-done.1, bf16[512,1,64]{2,0,1:T(8,128)(2,1)S(1)} %get-tuple-element.14, ...), kind=kOutput, calls=%fused_computation.4 | convolution fusion | flops 1089204224 | bytes 18628608 | tf_op jit(solution)/shard_map/qkgd,skd->qkgs/dot_general | solution.py:44
  519.3 0.0 copy-start.4
  519.3 9.3 %fusion = f32[512,8]{0,1:T(8,128)S(1)} fusion(f32[1024,512,8]{1,0,2:T(8,128)} %get-tuple-element.32, f32[512,8]{0,1:T(8,128)S(1)} %get-tuple-element.31, pred[512,1024]{0,1:T(8,128)(4,1)S(1)} %copy-done), kind=kLoop, calls=%fused_computation.2 | loop fusion | flops 16773120 | bytes 17334272 | tf_op jit(solution)/shard_map/reduce_sum | solution.py:50
  528.6 0.3 fusion.89
  529.0 9.1 %fusion.10 = bf16[1,128,512,8]{2,1,3,0:T(8,128)(2,1)S(1)} fusion(f32[1024,512,8]{1,0,2:T(8,128)} %get-tuple-element.32, f32[512,8]{0,1:T(8,128)S(1)} %get-tuple-element.31, pred[512,1024]{0,1:T(8,128)(4,1)S(1)} %copy-done, f32[512,8]{0,1:T(8,128)S(1)} %fusion, bf16[512,1,128]{2,0,1:T(8,128)(2,1)S(1)} %copy-done.4, bf16[512,1,128]{2,0,1:T(8,128)(2,1)S(1)} %copy-done.10), kind=kOutput, calls=%fused_computation.14 | convolution fusion | flops 1092091904 | bytes 18644992 | tf_op jit(solution)/shard_map/qkgs,skd->qkgd/dot_general | solution.py:51
  538.1 0.1 fusion.48
  538.2 1.3 copy.29
  539.5 72.5 %psum.31 = f32[64,1,8]{0,2,1:T(8,128)S(1)} all-reduce(f32[64,1,8]{0,2,1:T(8,128)S(1)} %copy-done.8), channel_id=1, replica_groups=mesh['ctx'=32,'tp'=8] {'ctx'}, use_global_device_ids=true, to_apply=%region_9.10 | all-reduce | flops 512 | bytes 4096 | tf_op jit(solution)/shard_map/psum | solution.py:148
  612.1 41.0 %all-reduce.5.cloned.1.call-done = f32[64,1,8,128]{3,0,2,1:T(8,128)} async-done(((f32[64,1,8,128]{3,0,2,1:T(8,128)}), f32[64,1,8,128]{3,0,2,1:T(8,128)}) %all-reduce.5.cloned.1.call-update) | async-done | bytes 262160 | tf_op jit(solution)/shard_map/psum | solution.py:148
  653.1 1.3 fusion.23
  654.4 0.1 copy.28
  654.5 0.7 copy.50
  (27 shorter events, 0.2 us)
Async XLA Ops:
  7.2 84.3 %all-gather.9.cloned.1.call-start = ((), (), s32[]{:S(2)}) async-start(), calls=%async_computation.2 | async-start | bytes 2162688 | tf_op jit(solution)/shard_map/all_gather | solution.py:99
  7.9 134.1 %all-gather.5.cloned.1.call-start = ((), (), s32[]{:S(2)}) async-start(), calls=%async_computation | async-start | bytes 9437184 | tf_op jit(solution)/shard_map/all_gather | solution.py:87
  8.6 214.9 %all-gather.7.cloned.1.call-start = ((), (), s32[]{:S(2)}) async-start(), calls=%async_computation.1 | async-start | bytes 2162688 | tf_op jit(solution)/shard_map/all_gather | solution.py:104
  9.4 354.5 %all-gather.11.cloned.1.call-start = ((), (), s32[]{:S(2)}) async-start(), calls=%async_computation.3 | async-start | bytes 17301504 | tf_op jit(solution)/shard_map/all_gather | solution.py:94
  10.0 498.6 %all-reduce.7.cloned.1.call-start = ((), (), s32[]{:S(2)}) async-start(), calls=%async_computation.5 | async-start | bytes 524288 | tf_op jit(solution)/shard_map/psum | solution.py:12
  10.0 1.6 collective-permute-start
  12.7 9.0 %collective-permute-start.1 = (bf16[64,2048]{1,0:T(8,128)(2,1)S(1)}, bf16[64,2048]{1,0:T(8,128)(2,1)S(1)}, u32[]{:S(2)}, u32[]{:S(2)}) collective-permute-start(bf16[64,2048]{1,0:T(8,128)(2,1)S(1)} %maximum_select_fusion.2), channel_id=1, source_target_pairs={{0,2},{1,3},{2,0},{3,1},{4,6},{5,7},{6,4},{7,5},{8,10},{9,11},{10,... | collective-permute-start | bytes 786440 | tf_op jit(solution)/shard_map/ppermute | solution.py:79
  21.8 15.1 %collective-permute-start.2 = (bf16[64,4096]{1,0:T(8,128)(2,1)S(1)}, bf16[64,4096]{1,0:T(8,128)(2,1)S(1)}, u32[]{:S(2)}, u32[]{:S(2)}) collective-permute-start(bf16[64,4096]{1,0:T(8,128)(2,1)S(1)} %maximum_select_fusion.1), channel_id=1, source_target_pairs={{0,4},{1,5},{2,6},{3,7},{4,0},{5,1},{6,2},{7,3},{8,12},{9,13},{10,... | collective-permute-start | bytes 1572872 | tf_op jit(solution)/shard_map/ppermute | solution.py:79
  37.1 112.1 %copy-start.9 = (f32[64]{0:T(128)S(1)}, f32[64]{0:T(128)}, u32[]{:S(2)}) copy-start(f32[64]{0:T(128)} %constant.33.clone) | copy-start | bytes 772
  150.4 79.7 %copy-start.1 = (bf16[512,1,64]{2,0,1:T(8,128)(2,1)}, bf16[512,1,64]{2,0,1:T(8,128)(2,1)S(1)}, u32[]{:S(2)}) copy-start(bf16[512,1,64]{2,0,1:T(8,128)(2,1)S(1)} %get-tuple-element.15) | copy-start | bytes 196612
  230.2 149.5 %copy-start.2 = (bf16[576,128]{1,0:T(8,128)(2,1)}, bf16[576,128]{1,0:T(8,128)(2,1)S(1)}, u32[]{:S(2)}) copy-start(bf16[576,128]{1,0:T(8,128)(2,1)S(1)} %fusion.22) | copy-start | bytes 442372
  231.0 422.1 %all-reduce.5.cloned.1.call-start = ((), (), s32[]{:S(2)}) async-start(), calls=%async_computation.4 | async-start | bytes 524288 | tf_op jit(solution)/shard_map/psum | solution.py:148
  453.8 2.5 copy-start.7
  453.8 3.1 copy-start.3
  508.6 10.7 %copy-start = (pred[512,1024]{0,1:T(8,128)(4,1)S(1)}, pred[512,1024]{0,1:T(8,128)(4,1)}, u32[]{:S(2)}) copy-start(pred[512,1024]{0,1:T(8,128)(4,1)} %concatenate.86) | copy-start | bytes 1572868
  519.3 9.3 %copy-start.5 = (bf16[64,64]{1,0:T(8,128)(2,1)S(1)}, bf16[64,64]{1,0:T(8,128)(2,1)}, u32[]{:S(2)}) copy-start(bf16[64,64]{1,0:T(8,128)(2,1)} %get-tuple-element.20) | copy-start | bytes 24580
  519.3 9.3 %copy-start.6 = (bf16[64,64]{1,0:T(8,128)(2,1)S(1)}, bf16[64,64]{1,0:T(8,128)(2,1)}, u32[]{:S(2)}) copy-start(bf16[64,64]{1,0:T(8,128)(2,1)} %get-tuple-element.21) | copy-start | bytes 24580
  519.3 9.6 %copy-start.4 = (bf16[512,1,128]{2,0,1:T(8,128)(2,1)S(1)}, bf16[512,1,128]{2,0,1:T(8,128)(2,1)}, u32[]{:S(2)}) copy-start(bf16[512,1,128]{2,0,1:T(8,128)(2,1)} %get-tuple-element.18) | copy-start | bytes 393220
  519.3 9.6 %copy-start.10 = (bf16[512,1,128]{2,0,1:T(8,128)(2,1)S(1)}, bf16[512,1,128]{2,0,1:T(8,128)(2,1)}, u32[]{:S(2)}) copy-start(bf16[512,1,128]{2,0,1:T(8,128)(2,1)} %get-tuple-element.7) | copy-start | bytes 393220
  529.0 10.6 %copy-start.8 = (f32[64,1,8]{0,2,1:T(8,128)S(1)}, f32[64,1,8]{0,2,1:T(8,128)}, u32[]{:S(2)}) copy-start(f32[64,1,8]{0,2,1:T(8,128)} %get-tuple-element.25) | copy-start | bytes 6148
Sparse Core Ops, SparseCore 0:
  10.6 80.8 all-gather.8
  93.3 48.6 all-gather.4
  144.6 78.9 all-gather.6
  226.0 137.7 all-gather.10
  367.2 141.3 all-reduce.6
  511.9 141.1 all-reduce.4
